TPU v7x, 128 devices: a whole 4x4x4 slice. The times are simulated.
128 devices in a mesh: box: 16 (over x, y), bal: 8 (over z, core).
Axes of the slice: x: 4, y: 4, z: 4, core: 2. Of those that a mesh axis runs over, the one named last changes fastest.
Arguments:
- species_state: bfloat16 [512, 218, 1024], P('box', None, 'bal'), may hold values from -6 to 6
- stiffness: int32 [512, 8], P('box', 'bal'), may hold values from 6 to 12
- send_list: int32 [16, 8, 16, 4], P('box', 'bal'), may hold values from -1 to 31, as said below
- jacobian: bfloat16 [1024, 8, 256, 256], P('box', 'bal'), may hold values from -0.375 to 0.375
- pattern: int32 [1024, 8, 4, 4], P('box', 'bal'), may hold values 0 or 1
- diffusivity: float32 [218], replicated, may hold values from 0.02 to 0.24
Outputs:
- species_field: float32 [512, 218, 1024], P('box', None, 'bal')
Inputs may be any that keep to these rules, and one draw needn't show every extreme that they name: `send_list`: in the table of device (b, j), entry (o, c) is the local tile that goes to slot c of owner o in the same j, or -1 for an empty slot. Every local tile stands exactly once in its device's table. In every j, one owner has all 4 slots from every device filled. Any slot of the other owners may be filled or empty.
All inputs are finite; a program needn't handle non-finite values. No bound on the sum of `pattern` on one device may be relied on, other than what follows from the above.
Results may differ from a plain program's by a relative error of at most 0.0003.
Values may be sent and summed in bfloat16 or wider, within the bound.
No kernel may reach another device: no remote copies, remote signals or barrier semaphores. Data moves between devices by JAX's collectives and lax.ppermute only.
A program may use at most 128 MiB of HBM per device.

v0:
```python
import functools

import jax
import numpy as np
import jax.numpy as jnp
from jax import lax
from jax.experimental import pallas as pl
from jax.experimental.pallas import tpu as pltpu
from jax.sharding import PartitionSpec as P

S = 218
SR = 224
SP = 256
BL = 64
NB = 4
PACK = 400
LANES = 128
EPSILON = 1e-06
GROUP = 8
SLOTS = 4
CHUNKS = ((0, 3), (3, 1))
PACK_BOXES = 8
TURN_SPECIES = 112
SPECIES = 56
WIDE_VMEM = 61 * 1024 * 1024
INNER_VMEM = 48 * 1024 * 1024
TIGHT_VMEM = 40 * 1024 * 1024


def lane_iota(rows):
    return lax.broadcasted_iota(jnp.int32, (rows, LANES), 1)


def make_plan(table, counts):
    slots, boxes = table.shape
    tiles = counts.shape[1]
    size = float(LANES)
    filler = jnp.full((slots, LANES - boxes), -1.0, jnp.float32)
    spread = jnp.concatenate([table.astype(jnp.float32), filler], axis=1)
    counts = jnp.concatenate(
        [counts.astype(jnp.float32), jnp.zeros((1, LANES - tiles), jnp.float32)], axis=1
    )
    lane = lane_iota(LANES).astype(jnp.float32)
    item = lax.broadcasted_iota(jnp.int32, (LANES, LANES), 0).astype(jnp.float32)
    row = jnp.full((1, LANES), -1.0, jnp.float32)
    for slot in range(slots):
        part = pltpu.roll(spread, slot * boxes, 1)[slot : slot + 1] if slot else spread[0:1]
        here = (lane_iota(1) >= slot * boxes) & (lane_iota(1) < (slot + 1) * boxes)
        row = jnp.where(here, part, row)
    tile = jnp.transpose(jnp.broadcast_to(row, (LANES, LANES)))
    turns = jnp.sum(jnp.where(tile == lane, counts, 0.0), axis=1, keepdims=True)
    turns = jnp.broadcast_to(turns, (LANES, LANES))
    live = tile >= 0.0
    early_size = CHUNKS[0][1] * boxes
    early = live & (item < early_size)
    weight = (size - turns) * size + item

    def rank(key):
        smaller = jnp.where(jnp.transpose(key) < key, 1.0, 0.0)
        return jnp.broadcast_to(jnp.sum(smaller, axis=1, keepdims=True), (LANES, LANES))

    late = 4.0 * size * size
    begun = jnp.sum(jnp.where(early, 1.0, 0.0), axis=0, keepdims=True)
    begun = jnp.floor(begun * (1.0 / GROUP)) * GROUP
    chosen = early & (rank(jnp.where(early, weight, late + item)) < begun)
    place = rank(weight + jnp.where(chosen, 0.0, jnp.where(live, late, 2.0 * late)))
    slot_of = jnp.floor(item * (1.0 / boxes))
    box_of = item - slot_of * boxes
    width = float(CHUNKS[0][1])
    source = jnp.where(item < early_size, box_of * width + slot_of, item)
    rows = [
        jnp.sum(jnp.where(place == lane, value, 0.0), axis=0, keepdims=True)
        for value in (source, tile, turns)
    ]
    rows += [begun, jnp.zeros((4, LANES), jnp.float32)]
    return jnp.concatenate(rows, axis=0).astype(jnp.int32)


def pack_kernel(pattern_ref, table_ref, counts_ref, diffusivity_ref, cells_ref, jac_ref,
                plan_ref, rate_ref, state_ref, *out_refs):
    @pl.when(pl.program_id(0) == 0)
    def _():
        plan_ref[...] = make_plan(table_ref[...], counts_ref[...])
        row = jnp.concatenate(
            [diffusivity_ref[...], jnp.zeros((1, SP - S), jnp.float32)], axis=1
        )
        for start in (0, LANES):
            rows = min(LANES, SR - start)
            part = jnp.broadcast_to(row[:, start : start + LANES], (LANES, LANES))
            rate_ref[start : start + rows, :] = jnp.transpose(part)[0:rows]

    state_ref[...] = cells_ref[...].astype(jnp.float32)

    low_half = lane_iota(1) < BL
    half_rows = SR // 2
    tail = SR - (NB - 1) * BL
    inside = lax.broadcasted_iota(jnp.int32, (tail, LANES), 0) < S - (NB - 1) * BL
    inside = inside.astype(jnp.float32).astype(jnp.bfloat16)
    middle_lane = lane_iota(half_rows)
    edge_lane = lane_iota(BL)

    def one_box(inner, carry):
        box = pl.program_id(0) * PACK_BOXES + inner
        for slot in range(SLOTS):
            chunk = next(k for k, (at, n) in enumerate(CHUNKS) if at <= slot < at + n)
            put = functools.partial(out_refs[chunk].__setitem__)
            place = slot - CHUNKS[chunk][0]
            held = box * SLOTS + slot
            right = []
            for p in range(NB):
                rows = min(SR, (p + 1) * BL) - p * BL
                parts = []
                for half in range(2):
                    mask = jnp.where(
                        low_half,
                        pattern_ref[p, 2 * half, held].astype(jnp.float32),
                        pattern_ref[p, 2 * half + 1, held].astype(jnp.float32),
                    ).astype(jnp.bfloat16)
                    value = (
                        jac_ref[inner, slot, p * BL : p * BL + rows, half * LANES : (half + 1) * LANES]
                        * mask
                    )
                    parts.append(value * inside if p == NB - 1 else value)
                put((inner, place, slice(p * BL, p * BL + rows), slice(None)), parts[0])
                right.append(parts[1])
            upper = jnp.concatenate([right[0], right[1][: half_rows - BL]], axis=0)
            lower = jnp.concatenate([right[1][half_rows - BL :], right[2], right[3]], axis=0)
            middle = jnp.where(middle_lane < BL, upper, pltpu.roll(lower, BL, 1))
            put((inner, place, slice(SR, SR + half_rows), slice(None)), middle)
            last = jnp.concatenate([right[3], jnp.zeros((BL - tail, LANES), jnp.bfloat16)], axis=0)
            edge = jnp.where(
                edge_lane < 64,
                jnp.where(edge_lane < 32, pltpu.roll(right[0], 64, 1), pltpu.roll(right[1], 96, 1)),
                jnp.where(edge_lane < 96, right[2], pltpu.roll(last, 32, 1)),
            )
            put((inner, place, slice(SR + half_rows, PACK), slice(None)), edge)
        return carry

    lax.fori_loop(0, PACK_BOXES, one_box, 0)


def pack_all(jacobian, pattern, table, counts, diffusivity, cells):
    boxes = jacobian.shape[0]
    tiles = cells.shape[1]
    last = (S - 1) // TURN_SPECIES
    return pl.pallas_call(
        pack_kernel,
        grid=(boxes // PACK_BOXES,),
        in_specs=[
            pl.BlockSpec(memory_space=pltpu.SMEM),
            pl.BlockSpec(table.shape, lambda b: (0, 0)),
            pl.BlockSpec(counts.shape, lambda b: (0, 0)),
            pl.BlockSpec(diffusivity.shape, lambda b: (0, 0)),
            pl.BlockSpec(
                (TURN_SPECIES, tiles, LANES), lambda b: (jnp.minimum(b, last), 0, 0)
            ),
            pl.BlockSpec((PACK_BOXES, SLOTS, SR, SP), lambda b: (b, 0, 0, 0)),
        ],
        out_specs=[
            pl.BlockSpec((8, LANES), lambda b: (0, 0)),
            pl.BlockSpec((SR, LANES), lambda b: (0, 0)),
            pl.BlockSpec(
                (TURN_SPECIES, tiles, LANES), lambda b: (jnp.minimum(b, last), 0, 0)
            ),
        ]
        + [
            pl.BlockSpec((PACK_BOXES, n, PACK, LANES), lambda b: (b, 0, 0, 0)) for _, n in CHUNKS
        ],
        out_shape=[
            jax.ShapeDtypeStruct((8, LANES), jnp.int32),
            jax.ShapeDtypeStruct((SR, LANES), jnp.float32),
            jax.ShapeDtypeStruct((S, tiles, LANES), jnp.float32),
        ]
        + [
            jax.ShapeDtypeStruct((boxes, n, PACK, LANES), jnp.bfloat16) for _, n in CHUNKS
        ],
        compiler_params=pltpu.CompilerParams(vmem_limit_bytes=WIDE_VMEM),
        name="pack_all",
    )(pattern, table, counts, diffusivity, cells, jacobian)


def unpack(packed_ref, item, dense_ref):
    half_rows = SR // 2
    dense_ref[:, 0:LANES] = packed_ref[item, pl.ds(0, SR), :]
    middle = packed_ref[item, pl.ds(SR, half_rows), :]
    edge = packed_ref[item, pl.ds(SR + half_rows, BL), :]
    high = pltpu.roll(middle, BL, 1)

    def put(row, rows, low, rest):
        dense_ref[pl.ds(row, rows), LANES:SP] = jnp.where(lane_iota(rows) < BL, low, rest)

    put(0, 64, middle[0:64], pltpu.roll(edge, 64, 1))
    shifted = pltpu.roll(edge, 32, 1)
    put(64, 48, middle[64:112], shifted[0:48])
    put(112, 16, high[0:16], shifted[48:64])
    put(128, 64, high[16:80], edge)
    put(192, 32, high[80:112], pltpu.roll(edge[0:32], 96, 1))


def solve_kernel(chunk, *refs):
    if chunk == 0:
        plan_ref, state_hbm, packed_hbm, out_hbm, rows_hbm, edge_ref = refs[:6]
        scratch = refs[6:]
    else:
        plan_ref, state_hbm, packed_hbm, second_hbm, _, _, edge_in = refs[:7]
        out_hbm, rows_hbm, edge_ref = refs[7:10]
        scratch = refs[10:]
    packed, state, outgoing, arrived, sent = scratch[:5]
    dense, right, left_over, mapped, guess, sums = (
        scratch[5 + GROUP * kind : 5 + GROUP * (kind + 1)] for kind in range(6)
    )
    tiles = state_hbm.shape[1]
    begun = plan_ref[3, 0]
    base = 0 if chunk == 0 else begun
    groups = (begun if chunk == 0 else tiles - begun) // GROUP

    def fetch(place, origin, at):
        return pltpu.make_async_copy(origin.at[at], packed.at[place], arrived.at[0, place])

    def fetch_state(place):
        tile = plan_ref[1, base + place]
        return pltpu.make_async_copy(
            state_hbm.at[:, tile, :], state.at[place, 0:S], arrived.at[1, place]
        )

    def start_fetch(place, carry):
        at = plan_ref[0, base + place]
        state[place, SR - 8 : SR, :] = jnp.zeros((8, LANES), jnp.float32)
        fetch_state(place).start()
        if chunk == 0:
            fetch(place, packed_hbm, at).start()
        else:
            early = packed_hbm.shape[0]

            @pl.when(at < early)
            def _():
                fetch(place, packed_hbm, at).start()

            @pl.when(at >= early)
            def _():
                fetch(place, second_hbm, at - early).start()

        return carry

    lax.fori_loop(0, groups * GROUP, start_fetch, 0)
    for member in range(GROUP):
        right[member][SR:SP, :] = jnp.zeros((SP - SR, SP), jnp.bfloat16)
    if chunk == 0:
        edge_ref[...] = jnp.zeros_like(edge_ref)
    else:
        edge_ref[...] = edge_in[...]
    edge_lane = lane_iota(SR) // 4

    def send(buffer, member, tile):
        return pltpu.make_async_copy(
            outgoing.at[buffer, member], out_hbm.at[tile], sent.at[buffer, member]
        )

    def send_row(buffer, member, tile):
        at = jnp.where(tile < 2, tile, tile - (tiles - 4))
        return pltpu.make_async_copy(
            outgoing.at[buffer, member], rows_hbm.at[at], sent.at[2 + buffer, member]
        )

    def is_row(tile):
        return (tile < 2) | (tile >= tiles - 2)

    def drain(group_no):
        for member in range(GROUP):
            tile = plan_ref[1, base + group_no * GROUP + member]
            send(group_no % 2, member, tile).wait()

            @pl.when(is_row(tile))
            def _():
                send_row(group_no % 2, member, tile).wait()

    def split(member, row, rows, remainder):
        high = remainder.astype(jnp.bfloat16)
        span = slice(row, row + rows)
        right[member][span, 0:LANES] = high
        right[member][span, LANES:SP] = (remainder - high.astype(jnp.float32)).astype(
            jnp.bfloat16
        )

    def multiply(member):
        return jnp.dot(
            dense[member][...], right[member][...], preferred_element_type=jnp.float32
        )

    def measure(member, product):
        above = jnp.zeros((8, LANES), jnp.float32)
        below = jnp.zeros((8, LANES), jnp.float32)
        for row in range(0, SR, 8):
            span = slice(row, row + 8)
            remainder = left_over[member][span, :]
            value = remainder - (product[span, 0:LANES] + product[span, LANES:SP])
            mapped[member][span, :] = value
            above = above + remainder * value
            below = below + value * value
        return above, below

    def move(member, above, below, active):
        above = jnp.sum(above, axis=0, keepdims=True)
        below = jnp.sum(below, axis=0, keepdims=True) + EPSILON
        step = jnp.where(active, above / below, 0.0)
        for row in range(0, SR, 16):
            span = slice(row, row + 16)
            remainder = left_over[member][span, :]
            guess[member][span, :] += step * remainder
            remainder = remainder - step * mapped[member][span, :]
            left_over[member][span, :] = remainder
            split(member, row, 16, remainder)

    def keep_sums(member, above, below):
        sums[member][0:8, :] = above
        sums[member][8:16, :] = below

    def one_group(group_no, carry):
        buffer = group_no % 2
        places = [group_no * GROUP + member for member in range(GROUP)]
        chosen = [plan_ref[1, base + place] for place in places]
        counts = [plan_ref[2, base + place] for place in places]

        for member in range(GROUP):
            fetch(places[member], packed_hbm, 0).wait()
            fetch_state(places[member]).wait()
        for member in range(GROUP):
            unpack(packed, places[member], dense[member])
            start_value = state[places[member]]
            right[member][0:SR, 0:LANES] = start_value.astype(jnp.bfloat16)
            guess[member][...] = start_value
        for member in range(GROUP):
            remainder = jnp.dot(
                dense[member][...],
                right[member][:, 0:LANES],
                preferred_element_type=jnp.float32,
            )
            left_over[member][...] = remainder
            split(member, 0, SR, remainder)

        half = GROUP // 2
        for member in range(half, GROUP):
            keep_sums(member, *measure(member, multiply(member)))

        def advance(turn_no, inner):
            for one, other in zip(range(half), range(half, GROUP)):
                product = multiply(one)
                move(other, sums[other][0:8, :], sums[other][8:16, :], turn_no < counts[other])
                next_product = multiply(other)
                move(one, *measure(one, product), turn_no < counts[one])
                keep_sums(other, *measure(other, next_product))
            return inner

        lax.fori_loop(0, functools.reduce(jnp.maximum, counts), advance, 0)

        @pl.when(group_no >= 2)
        def _():
            drain(group_no - 2)

        for member in range(GROUP):
            result = guess[member][...]
            outgoing[buffer, member] = result
            tile = chosen[member]
            edge_ref[...] = jnp.where(
                edge_lane == tile, pltpu.roll(result, (4 * tile + 2) % LANES, 1), edge_ref[...]
            )
            send(buffer, member, tile).start()

            @pl.when(is_row(tile))
            def _():
                send_row(buffer, member, tile).start()

        return carry

    lax.fori_loop(0, groups, one_group, 0)

    for back in range(2):
        @pl.when(groups > back)
        def _():
            drain(groups - 1 - back)

    edge_ref[S + 2 : SR, :] = jnp.ones((SR - S - 2, LANES), jnp.float32)


def solve_chunk(chunk, plan, state, packed, reacted, rows, edge):
    tiles = state.shape[1]
    out_shape = (
        jax.ShapeDtypeStruct((tiles, SR, LANES), jnp.float32),
        jax.ShapeDtypeStruct((4, SR, LANES), jnp.float32),
        jax.ShapeDtypeStruct((SR, LANES), jnp.float32),
    )
    anywhere = pl.BlockSpec(memory_space=pl.ANY)
    vmem = pl.BlockSpec(memory_space=pltpu.VMEM)
    in_specs = [pl.BlockSpec(memory_space=pltpu.SMEM), anywhere]
    in_specs += [anywhere] * (chunk + 1)
    operands = [plan, state, *packed[: chunk + 1]]
    aliases = {}
    if chunk:
        in_specs += [anywhere, anywhere, vmem]
        operands += [reacted, rows, edge]
        aliases = {4: 0, 5: 1}
    tile_values = pltpu.VMEM((SR, LANES), jnp.float32)
    return pl.pallas_call(
        functools.partial(solve_kernel, chunk),
        in_specs=in_specs,
        out_specs=(anywhere, anywhere, vmem),
        out_shape=out_shape,
        input_output_aliases=aliases,
        scratch_shapes=[
            pltpu.VMEM((tiles, PACK, LANES), jnp.bfloat16),
            pltpu.VMEM((tiles, SR, LANES), jnp.float32),
            pltpu.VMEM((2, GROUP, SR, LANES), jnp.float32),
            pltpu.SemaphoreType.DMA((2, tiles)),
            pltpu.SemaphoreType.DMA((4, GROUP)),
        ]
        + [pltpu.VMEM((SR, SP), jnp.bfloat16)] * GROUP
        + [pltpu.VMEM((SP, SP), jnp.bfloat16)] * GROUP
        + [tile_values] * (3 * GROUP)
        + [pltpu.VMEM((16, LANES), jnp.float32)] * GROUP,
        compiler_params=pltpu.CompilerParams(vmem_limit_bytes=WIDE_VMEM),
        cost_estimate=pl.CostEstimate(
            flops=16 * 300_000_000, bytes_accessed=16 * 200000, transcendentals=0
        ),
        name="solve_chunk",
    )(*operands)


def is_odd(axis):
    return lax.rem(lax.axis_index(axis), 2) == 1


def message_kernel(rows_ref, near_ref, far_ref, near_out_ref, far_out_ref):
    tiles = LANES // 4
    lanes = lane_iota(SR)
    odd = is_odd("bal")
    low = jnp.where(odd, near_ref[...], far_ref[...])
    high = jnp.where(odd, far_ref[...], near_ref[...])
    odd = is_odd("box")

    def message(start, row, near):
        for to_near, out_ref in ((near, near_out_ref), (jnp.logical_not(near), far_out_ref)):

            @pl.when(to_near)
            def _():
                out_ref[0:2] = rows_ref[start : start + 2].astype(jnp.bfloat16)
                cells = jnp.where(
                    lanes == 0,
                    pltpu.roll(low, (-(4 * row + 1)) % LANES, 1),
                    pltpu.roll(high, (-(4 * row + 3)) % LANES, 1),
                )
                out_ref[2] = jnp.where(lanes == 2, 1.0, cells).astype(jnp.bfloat16)

    message(0, 0, odd)
    message(2, tiles - 1, jnp.logical_not(odd))


def make_messages(rows, near, far):
    vmem = pl.BlockSpec(memory_space=pltpu.VMEM)
    shape = jax.ShapeDtypeStruct((3, SR, LANES), jnp.bfloat16)
    return pl.pallas_call(
        message_kernel,
        in_specs=[vmem, vmem, vmem],
        out_specs=(vmem, vmem),
        out_shape=(shape, shape),
        compiler_params=pltpu.CompilerParams(vmem_limit_bytes=TIGHT_VMEM),
        name="make_messages",
    )(rows, near, far)


def beside(value, lanes):
    return jnp.where(lanes == 0, 0.0, pltpu.roll(value, 1, 1)) + jnp.where(
        lanes == LANES - 1, 0.0, pltpu.roll(value, LANES - 1, 1)
    )


def inner_kernel(tiles, block_ref, rate_ref, both_ref, out_ref):
    zero = jnp.zeros((1, 8, LANES), jnp.float32)

    def around(value, by):
        gap = jnp.concatenate([zero] * by, axis=0)
        return jnp.concatenate([gap, value[: tiles - by]], axis=0) + jnp.concatenate(
            [value[by:], gap], axis=0
        )

    for number in range(SPECIES // 8):
        span = slice(number * 8, number * 8 + 8)
        rate = rate_ref[span, :]
        keep = 1.0 - 4.0 * rate
        square = rate * rate
        cells = block_ref[:, span, :]
        flat = cells.reshape(tiles * 8, LANES)
        high = flat.astype(jnp.bfloat16)
        low = (flat - high.astype(jnp.float32)).astype(jnp.bfloat16)
        product = jnp.dot(
            jnp.concatenate([high, low], axis=1), both_ref[...], preferred_element_type=jnp.float32
        )
        once = product[:, 0:LANES].reshape(tiles, 8, LANES)
        twice = product[:, LANES:].reshape(tiles, 8, LANES)
        near = (2.0 * keep * rate) * (around(cells, 1) + once)
        sides = around(once, 1)
        far = square * ((around(cells, 2) + twice) + (sides + sides))
        own = keep * keep + 2.0 * square
        end = keep * keep + square
        value = near + far
        out_ref[1 : tiles - 1, span, :] = value[1 : tiles - 1] + own * cells[1 : tiles - 1]
        out_ref[0, span, :] = value[0] + end * cells[0]
        out_ref[tiles - 1, span, :] = value[tiles - 1] + end * cells[tiles - 1]


def diffuse_inside(block, rate):
    tiles = block.shape[0]
    cells = pl.BlockSpec((tiles, SPECIES, LANES), lambda g: (0, g, 0))
    place = np.arange(LANES)
    next_to = (np.abs(place[:, None] - place[None, :]) == 1).astype(np.float32)
    both = np.concatenate([next_to, next_to @ next_to], axis=1)
    both = jnp.asarray(np.concatenate([both, both], axis=0), jnp.bfloat16)
    return pl.pallas_call(
        functools.partial(inner_kernel, tiles),
        grid=(SR // SPECIES,),
        in_specs=[
            cells,
            pl.BlockSpec((SPECIES, LANES), lambda g: (g, 0)),
            pl.BlockSpec((2 * LANES, 2 * LANES), lambda g: (0, 0)),
        ],
        out_specs=cells,
        out_shape=jax.ShapeDtypeStruct(block.shape, jnp.float32),
        compiler_params=pltpu.CompilerParams(vmem_limit_bytes=INNER_VMEM),
        cost_estimate=pl.CostEstimate(
            flops=tiles * SR * LANES * 20, bytes_accessed=8 * block.size, transcendentals=0
        ),
        name="diffuse_inside",
    )(block, rate, both)


def border_kernel(tiles, inner_ref, top_ref, bottom_ref, near_row_ref, far_row_ref, near_ref,
                  far_ref, near_here_ref, far_here_ref, own_ref, rate_ref, out_ref):
    lanes = lane_iota(8)
    column = lanes % 4
    here = S + 2 - (SR - 8)
    from_near = (column < 2) == is_odd("bal")
    near_above = is_odd("box")
    has_side = jnp.where(
        from_near, near_here_ref[here : here + 1, :], far_here_ref[here : here + 1, :]
    )
    near_edge = (lanes < 2) | (lanes >= LANES - 2)

    def slab(number):
        span = slice(number * 8, number * 8 + 8)
        overall = pl.program_id(0) * (SPECIES // 8) + number
        wide = pl.ds(pl.multiple_of(overall // 2 * 16, 16), 16)

        def read(ref, row):
            both = ref[row, wide, :].astype(jnp.float32)
            return jnp.where(overall % 2 == 0, both[0:8], both[8:16])

        near_rows = [read(near_row_ref, row) for row in range(3)]
        far_rows = [read(far_row_ref, row) for row in range(3)]
        above = [jnp.where(near_above, a, b) for a, b in zip(near_rows, far_rows)]
        below = [jnp.where(near_above, b, a) for a, b in zip(near_rows, far_rows)]

        rate = rate_ref[span, :]
        keep = 1.0 - 4.0 * rate
        own = own_ref[span, :]
        ghost = jnp.where(from_near, near_ref[span, :], far_ref[span, :])

        def rows_beside(near, far, inner, corner):
            exists = jnp.broadcast_to(corner[:, 2:3], (8, LANES))
            left = jnp.where(lanes == 0, corner, pltpu.roll(near, 1, 1))
            right = jnp.where(lanes == LANES - 1, corner, pltpu.roll(near, LANES - 1, 1))
            later = (keep * near + rate * ((far + inner) + (left + right))) * exists
            first = rate * near
            outer = keep * first + rate * (beside(first, lanes) + later)
            return outer, rate * first

        corner_above, corner_below = above[2], below[2]
        row_terms = {}
        row_terms[0], row_terms[1] = rows_beside(
            above[1], above[0], top_ref[0, span, :], corner_above
        )
        row_terms[tiles - 1], row_terms[tiles - 2] = rows_beside(
            below[0], below[1], bottom_ref[0, span, :], corner_below
        )

        up = pltpu.roll(ghost, 4, 1)
        up = jnp.where(lanes == 1, pltpu.roll(corner_above, 1, 1), up)
        up = jnp.where(lanes == 2, pltpu.roll(corner_above, 3, 1), up)
        down = pltpu.roll(ghost, LANES - 4, 1)
        down = jnp.where(lanes == LANES - 3, pltpu.roll(corner_below, LANES - 3, 1), down)
        down = jnp.where(lanes == LANES - 2, pltpu.roll(corner_below, LANES - 1, 1), down)
        side = jnp.where(
            column == 1,
            pltpu.roll(own, LANES - 1, 1) + pltpu.roll(ghost, 1, 1),
            pltpu.roll(own, 1, 1) + pltpu.roll(ghost, LANES - 1, 1),
        )
        later = (keep * ghost + rate * ((up + down) + side)) * has_side
        first = rate * ghost
        first_up = jnp.where(lanes < 4, 0.0, pltpu.roll(first, 4, 1))
        first_down = jnp.where(lanes >= LANES - 4, 0.0, pltpu.roll(first, LANES - 4, 1))
        outer = keep * first + rate * ((first_up + first_down) + later)
        second = rate * first
        terms = jnp.where(
            column < 2,
            jnp.where(column == 0, pltpu.roll(second, LANES - 2, 1), pltpu.roll(outer, LANES - 1, 1)),
            jnp.where(column == 2, pltpu.roll(outer, 1, 1), pltpu.roll(second, 2, 1)),
        )
        values = []
        for row in range(tiles):
            value = inner_ref[row, span, :] + jnp.where(
                near_edge, pltpu.roll(terms, (-(4 * row + 2)) % LANES, 1), 0.0
            )
            if row in row_terms:
                value = value + row_terms[row]
            values.append(value)
        out_ref[span, :, :] = jnp.swapaxes(jnp.stack(values, axis=0), 0, 1)

    for number in range(SPECIES // 8):
        slab(number)


def add_borders(inner, rows, near_row, far_row, near, far, own, rate):
    tiles = inner.shape[0]
    message = pl.BlockSpec((3, SR, LANES), lambda g: (0, 0, 0))
    edge = pl.BlockSpec((SPECIES, LANES), lambda g: (g, 0))
    flags = pl.BlockSpec((8, LANES), lambda g: (SR // 8 - 1, 0))
    return pl.pallas_call(
        functools.partial(border_kernel, tiles),
        grid=(SR // SPECIES,),
        in_specs=[
            pl.BlockSpec((tiles, SPECIES, LANES), lambda g: (0, g, 0)),
            pl.BlockSpec((1, SPECIES, LANES), lambda g: (0, g, 0)),
            pl.BlockSpec((1, SPECIES, LANES), lambda g: (3, g, 0)),
            message,
            message,
            edge,
            edge,
            flags,
            flags,
            edge,
            edge,
        ],
        out_specs=pl.BlockSpec((SPECIES, tiles, LANES), lambda g: (g, 0, 0)),
        out_shape=jax.ShapeDtypeStruct((S, tiles, LANES), jnp.float32),
        compiler_params=pltpu.CompilerParams(vmem_limit_bytes=TIGHT_VMEM),
        name="add_borders",
    )(inner, rows, rows, near_row, far_row, near, far, near, far, own, rate)


def trade(near_value, far_value, axis):
    count = lax.axis_size(axis)
    near = [(i, i ^ 1) for i in range(count) if i ^ 1 < count]
    far = [(i, j) for i in range(count) for j in [i + 1 if i % 2 else i - 1] if 0 <= j < count]
    return lax.ppermute(near_value, axis, near), lax.ppermute(far_value, axis, far)


def on_device(species_state, stiffness, send_list, jacobian, pattern, diffusivity):
    boxes = lax.axis_size("box")
    tiles = species_state.shape[0]
    slots = jacobian.shape[0] // boxes
    by_box = jacobian.reshape(boxes, slots, SP, SP)
    counts = stiffness.reshape(1, tiles)
    table = send_list.transpose(0, 1, 3, 2).reshape(slots, boxes)
    by_block = pattern.transpose(1, 2, 3, 0).reshape(NB, NB, boxes * slots)
    plan, rate, state, first, second = pack_all(
        by_box, by_block, table, counts, diffusivity.reshape(1, S), species_state.transpose(1, 0, 2)
    )
    plan, rate, state, first, second = lax.optimization_barrier(
        (plan, rate, state, first, second)
    )

    def exchange(packed):
        arrived = lax.all_to_all(packed, "box", split_axis=0, concat_axis=0, tiled=True)
        return arrived.reshape(-1, PACK, LANES)

    first = exchange(first)
    plan, rate, state, first, second = lax.optimization_barrier(
        (plan, rate, state, first, second)
    )
    second = exchange(second)
    early, rows, edge = solve_chunk(0, plan, state, (first, second), None, None, None)
    reacted, rows, edge = solve_chunk(1, plan, state, (first, second), early, rows, edge)

    near, far = trade(edge, edge, "bal")
    near_row, far_row = trade(*make_messages(rows, near, far), "box")
    inner = diffuse_inside(reacted, rate)
    field = add_borders(inner, rows, near_row, far_row, near, far, edge, rate)
    return field.transpose(1, 0, 2)


def solution(mesh):
    in_specs = (
        P("box", None, "bal"),
        P("box", "bal"),
        P("box", "bal", None, None),
        P("box", "bal", None, None),
        P("box", "bal", None, None),
        P(),
    )
    return jax.shard_map(
        on_device,
        mesh=mesh,
        in_specs=in_specs,
        out_specs=P("box", None, "bal"),
        check_vma=False,
    )
```

profile of v0, /device:TPU:66, one launch (start us, length us, event | category | flops | bytes accessed | tf_op | source)
XLA Modules:
  0.0 144.5 jit_solution(448819627967751327)
XLA Ops:
  0.0 8.4 %pack_all.1 = (s32[8,128]{1,0:T(8,128)}, f32[224,128]{1,0:T(8,128)}, f32[218,32,128]{2,1,0:T(8,128)}, bf16[16,3,400,128]{3,2,1,0:T(8,128)(2,1)}, bf16[16,1,400,128]{3,2,1,0:T(8,128)(2,1)}) custom-call(s32[4,4,64]{2,1,0:T(4,128)} %bitcast.18, s32[4,16]{1,0:T(4,128)} %bitcast.19, s32[1,32]{1,0:T(1,128)} %bitcast.21, f32[1,218]{1,0:T(1,128)} %bitcast.20, ...), custom_call_target="tpu_custom_call" | custom-call | tf_op jit(solution)/shard_map/pack_all/pallas_call | solution.py:146
  8.4 65.1 %all_to_all.10 = bf16[16,3,400,128]{3,2,1,0:T(8,128)(2,1)} all-to-all(bf16[16,3,400,128]{3,2,1,0:T(8,128)(2,1)} %get-tuple-element.26), channel_id=1, replica_groups=mesh['box'=16,'bal'=8] {'box'}, dimensions={0} | all-to-all | bytes 9830400 | tf_op jit(solution)/shard_map/all_to_all | solution.py:671
  73.5 5.2 %all-to-all-start.1 = ((bf16[16,1,400,128]{3,2,1,0:T(8,128)(2,1)}), bf16[16,1,400,128]{3,2,1,0:T(8,128)(2,1)S(1)}, u32[]{:S(2)}, u32[]{:S(2)}) async-start(bf16[16,1,400,128]{3,2,1,0:T(8,128)(2,1)} %get-tuple-element.31), calls=%async_computation.1 | async-start | bytes 3276800 | tf_op jit(solution)/shard_map/all_to_all | solution.py:671
  78.7 19.6 %solve_chunk.2 = (f32[32,224,128]{2,1,0:T(8,128)}, f32[4,224,128]{2,1,0:T(8,128)}, f32[224,128]{1,0:T(8,128)}) custom-call(s32[8,128]{1,0:T(8,128)} %get-tuple-element.28.refs_0_, f32[218,32,128]{2,1,0:T(8,128)} %get-tuple-element.29.refs_1_, bf16[48,400,128]{2,1,0:T(8,128)(2,1)} %bitcast.14), custom_call_target="tpu_custom_call" | custom-call | flops 4800000000 | bytes 3200000 | tf_op jit(solution)/shard_map/solve_chunk/pallas_call | solution.py:403
  98.3 1.2 all-to-all-done.1
  99.5 0.0 copy-start.5
  99.5 1.2 copy-done.5
  100.7 0.0 copy-start.2
  100.7 0.0 copy-start.3
  100.7 9.8 %solve_chunk.3 = (f32[32,224,128]{2,1,0:T(8,128)}, f32[4,224,128]{2,1,0:T(8,128)}, f32[224,128]{1,0:T(8,128)}) custom-call(s32[8,128]{1,0:T(8,128)} %get-tuple-element.28.refs_0_, f32[218,32,128]{2,1,0:T(8,128)} %get-tuple-element.29.refs_1_, bf16[48,400,128]{2,1,0:T(8,128)(2,1)} %bitcast.15, ...), custom_call_target="tpu_custom_call", output_to_operand_aliasing={{0}: (4, {}), {1}: (5, {})} | custom-call | flops 4800000000 | bytes 3200000 | tf_op jit(solution)/shard_map/solve_chunk/pallas_call | solution.py:403
  110.6 6.4 %collective-permute-start.1 = (f32[224,128]{1,0:T(8,128)}, f32[224,128]{1,0:T(8,128)S(1)}, u32[]{:S(2)}, u32[]{:S(2)}) collective-permute-start(f32[224,128]{1,0:T(8,128)} %get-tuple-element.38.own_ref), channel_id=1, source_target_pairs={{1,2},{2,1},{3,4},{4,3},{5,6},{6,5},{9,10},{10,9},{11,12},{12,11},... | collective-permute-start | bytes 344072 | tf_op jit(solution)/shard_map/ppermute | solution.py:652
  117.0 4.3 %collective-permute-start = (f32[224,128]{1,0:T(8,128)}, f32[224,128]{1,0:T(8,128)S(1)}, u32[]{:S(2)}, u32[]{:S(2)}) collective-permute-start(f32[224,128]{1,0:T(8,128)} %get-tuple-element.38.own_ref), channel_id=1, source_target_pairs={{0,1},{1,0},{2,3},{3,2},{4,5},{5,4},{6,7},{7,6},{8,9},{9,8},{10,11... | collective-permute-start | bytes 344072 | tf_op jit(solution)/shard_map/ppermute | solution.py:652
  121.3 0.0 collective-permute-done.1.far_ref.far_here_ref
  121.3 1.2 collective-permute-done.near_ref.near_here_ref
  122.5 0.0 copy-start
  122.5 1.0 copy-done
  123.5 0.2 make_messages.1
  123.7 6.0 %collective-permute-start.2 = (bf16[3,224,128]{2,1,0:T(8,128)(2,1)S(1)}, bf16[3,224,128]{2,1,0:T(8,128)(2,1)S(1)}, u32[]{:S(2)}, u32[]{:S(2)}) collective-permute-start(bf16[3,224,128]{2,1,0:T(8,128)(2,1)S(1)} %get-tuple-element.39), channel_id=1, source_target_pairs={{0,8},{8,0},{16,24},{24,16},{32,40},{40,32},{48,56},{56,48},{64,72... | collective-permute-start | bytes 516104 | tf_op jit(solution)/shard_map/ppermute | solution.py:652
  129.7 1.9 %collective-permute-start.3 = (bf16[3,224,128]{2,1,0:T(8,128)(2,1)S(1)}, bf16[3,224,128]{2,1,0:T(8,128)(2,1)S(1)}, u32[]{:S(2)}, u32[]{:S(2)}) collective-permute-start(bf16[3,224,128]{2,1,0:T(8,128)(2,1)S(1)} %get-tuple-element.40), channel_id=1, source_target_pairs={{8,16},{16,8},{24,32},{32,24},{40,48},{48,40},{56,64},{64,56},{72,... | collective-permute-start | bytes 516104 | tf_op jit(solution)/shard_map/ppermute | solution.py:652
  131.6 0.0 copy-done.2
  131.6 0.0 copy-done.3
  131.6 0.0 copy-start.1
  131.6 0.0 copy-start.4
  131.6 4.4 %diffuse_inside.1.inner_ref = f32[32,224,128]{2,1,0:T(8,128)S(1)} custom-call(f32[32,224,128]{2,1,0:T(8,128)} %get-tuple-element.35.block_ref, f32[224,128]{1,0:T(8,128)S(1)} %copy-done.2, bf16[256,256]{1,0:T(8,128)(2,1)S(1)} %copy-done.3), custom_call_target="tpu_custom_call" | custom-call | flops 18350080 | bytes 7340032 | tf_op jit(solution)/shard_map/diffuse_inside/pallas_call | solution.py:517
  136.1 0.0 collective-permute-done.2.near_row_ref
  136.1 3.0 %collective-permute-done.3.far_row_ref = bf16[3,224,128]{2,1,0:T(8,128)(2,1)S(1)} collective-permute-done((bf16[3,224,128]{2,1,0:T(8,128)(2,1)S(1)}, bf16[3,224,128]{2,1,0:T(8,128)(2,1)S(1)}, u32[]{:S(2)}, u32[]{:S(2)}) %collective-permute-start.3) | collective-permute-done | bytes 172064 | tf_op jit(solution)/shard_map/ppermute | solution.py:652
  139.1 0.0 copy-done.1
  139.1 0.0 copy-done.4
  139.1 5.4 %add_borders.1 = f32[218,32,128]{2,1,0:T(8,128)} custom-call(f32[32,224,128]{2,1,0:T(8,128)S(1)} %diffuse_inside.1.inner_ref, f32[4,224,128]{2,1,0:T(8,128)S(1)} %copy-done.1, f32[4,224,128]{2,1,0:T(8,128)S(1)} %copy-done.1, bf16[3,224,128]{2,1,0:T(8,128)(2,1)S(1)} %collective-permute-done.2.near_row_ref, ...), custom_call_target="tpu_custom_call" | custom-call | tf_op jit(solution)/shard_map/add_borders/pallas_call | solution.py:625
Async XLA Ops:
  73.5 26.0 %all-to-all-start.1 = ((bf16[16,1,400,128]{3,2,1,0:T(8,128)(2,1)}), bf16[16,1,400,128]{3,2,1,0:T(8,128)(2,1)S(1)}, u32[]{:S(2)}, u32[]{:S(2)}) async-start(bf16[16,1,400,128]{3,2,1,0:T(8,128)(2,1)} %get-tuple-element.31), calls=%async_computation.1 | async-start | bytes 3276800 | tf_op jit(solution)/shard_map/all_to_all | solution.py:671
  99.5 1.2 copy-start.5
  100.7 30.9 %copy-start.2 = (f32[224,128]{1,0:T(8,128)S(1)}, f32[224,128]{1,0:T(8,128)}, u32[]{:S(2)}) copy-start(f32[224,128]{1,0:T(8,128)} %get-tuple-element.36.rate_ref) | copy-start | bytes 344068
  100.7 30.9 %copy-start.3 = (bf16[256,256]{1,0:T(8,128)(2,1)S(1)}, bf16[256,256]{1,0:T(8,128)(2,1)}, u32[]{:S(2)}) copy-start(bf16[256,256]{1,0:T(8,128)(2,1)} %constant.2.clone.both_ref) | copy-start | bytes 393220
  110.6 10.7 %collective-permute-start.1 = (f32[224,128]{1,0:T(8,128)}, f32[224,128]{1,0:T(8,128)S(1)}, u32[]{:S(2)}, u32[]{:S(2)}) collective-permute-start(f32[224,128]{1,0:T(8,128)} %get-tuple-element.38.own_ref), channel_id=1, source_target_pairs={{1,2},{2,1},{3,4},{4,3},{5,6},{6,5},{9,10},{10,9},{11,12},{12,11},... | collective-permute-start | bytes 344072 | tf_op jit(solution)/shard_map/ppermute | solution.py:652
  117.0 5.5 %collective-permute-start = (f32[224,128]{1,0:T(8,128)}, f32[224,128]{1,0:T(8,128)S(1)}, u32[]{:S(2)}, u32[]{:S(2)}) collective-permute-start(f32[224,128]{1,0:T(8,128)} %get-tuple-element.38.own_ref), channel_id=1, source_target_pairs={{0,1},{1,0},{2,3},{3,2},{4,5},{5,4},{6,7},{7,6},{8,9},{9,8},{10,11... | collective-permute-start | bytes 344072 | tf_op jit(solution)/shard_map/ppermute | solution.py:652
  122.5 1.0 copy-start
  123.7 12.3 %collective-permute-start.2 = (bf16[3,224,128]{2,1,0:T(8,128)(2,1)S(1)}, bf16[3,224,128]{2,1,0:T(8,128)(2,1)S(1)}, u32[]{:S(2)}, u32[]{:S(2)}) collective-permute-start(bf16[3,224,128]{2,1,0:T(8,128)(2,1)S(1)} %get-tuple-element.39), channel_id=1, source_target_pairs={{0,8},{8,0},{16,24},{24,16},{32,40},{40,32},{48,56},{56,48},{64,72... | collective-permute-start | bytes 516104 | tf_op jit(solution)/shard_map/ppermute | solution.py:652
  129.7 9.4 %collective-permute-start.3 = (bf16[3,224,128]{2,1,0:T(8,128)(2,1)S(1)}, bf16[3,224,128]{2,1,0:T(8,128)(2,1)S(1)}, u32[]{:S(2)}, u32[]{:S(2)}) collective-permute-start(bf16[3,224,128]{2,1,0:T(8,128)(2,1)S(1)} %get-tuple-element.40), channel_id=1, source_target_pairs={{8,16},{16,8},{24,32},{32,24},{40,48},{48,40},{56,64},{64,56},{72,... | collective-permute-start | bytes 516104 | tf_op jit(solution)/shard_map/ppermute | solution.py:652
  131.6 7.5 %copy-start.1 = (f32[4,224,128]{2,1,0:T(8,128)S(1)}, f32[4,224,128]{2,1,0:T(8,128)}, u32[]{:S(2)}) copy-start(f32[4,224,128]{2,1,0:T(8,128)} %get-tuple-element.37.rows_ref.top_ref.bottom_ref) | copy-start | bytes 1376260
  131.6 7.5 %copy-start.4 = (f32[224,128]{1,0:T(8,128)S(1)}, f32[224,128]{1,0:T(8,128)}, u32[]{:S(2)}) copy-start(f32[224,128]{1,0:T(8,128)} %get-tuple-element.38.own_ref) | copy-start | bytes 344068
where the time goes:
time: 146 us; the launch traced here: 144 us
  blocking collectives  65.1 us (45%)
  Pallas kernels  47.8 us (33%)
  starting transfers between devices  23.8 us (16%)
  waiting for transfers between devices  5.41 us (4%)
  local copies, waits for them, and re-layouts  2.26 us (2%)
    all_to_all x1, blocking collectives, exchange(): lax.all_to_all(packed, 'box', split_axis=0, concat_axis=0, tiled=True)  65.1 us
    pallas_call x2, Pallas kernels, solve_chunk(): pl.pallas_call(functools.partial(solve_kernel, chunk), in_specs=in_specs,...  29.4 us
    ppermute x2, starting transfers between devices, trade(): lax.ppermute(near_value, axis, near)  10.2 us
    pallas_call x1, Pallas kernels, pack_all(): pl.pallas_call(pack_kernel, grid=(boxes // PACK_BOXES,), in_specs=[pl.Blo...  8.39 us
    ppermute x2, starting transfers between devices, trade(): lax.ppermute(far_value, axis, far)  8.33 us
    pallas_call x1, Pallas kernels, add_borders(): pl.pallas_call(functools.partial(border_kernel, tiles), grid=(SR // SPECI...  5.38 us
    all_to_all x1, starting transfers between devices, exchange(): lax.all_to_all(packed, 'box', split_axis=0, concat_axis=0, tiled=True)  5.22 us
    pallas_call x1, Pallas kernels, diffuse_inside(): pl.pallas_call(functools.partial(inner_kernel, tiles), grid=(SR // SPECIE...  4.42 us
  transfers between devices with their start and end apart: 5, of which 3 were waited for; matrix products, arithmetic and copies ran while one was open for 0% of the time, Pallas kernels for 17%

commit v1 on v0

--- a/solution.py
+++ b/solution.py
@@ -22,7 +22,7 @@
 PACK_BOXES = 8
 TURN_SPECIES = 112
 SPECIES = 56
-WIDE_VMEM = 61 * 1024 * 1024
+WIDE_VMEM = 63 * 1024 * 1024
 INNER_VMEM = 48 * 1024 * 1024
 TIGHT_VMEM = 40 * 1024 * 1024
 
@@ -136,7 +136,7 @@
             put((inner, place, slice(SR + half_rows, PACK), slice(None)), edge)
         return carry
 
-    lax.fori_loop(0, PACK_BOXES, one_box, 0)
+    lax.fori_loop(0, PACK_BOXES, one_box, 0, unroll=4)
 
 
 def pack_all(jacobian, pattern, table, counts, diffusivity, cells):
@@ -442,7 +442,7 @@
 
             @pl.when(to_near)
             def _():
-                out_ref[0:2] = rows_ref[start : start + 2].astype(jnp.bfloat16)
+                out_ref[0:2] = rows_ref[start : start + 2]
                 cells = jnp.where(
                     lanes == 0,
                     pltpu.roll(low, (-(4 * row + 1)) % LANES, 1),
@@ -473,8 +473,16 @@
     )
 
 
-def inner_kernel(tiles, block_ref, rate_ref, both_ref, out_ref):
+def inner_kernel(tiles, block_hbm, rate_ref, both_ref, out_ref, block_ref, arrived):
     zero = jnp.zeros((1, 8, LANES), jnp.float32)
+    copies = [
+        pltpu.make_async_copy(
+            block_hbm.at[:, at : at + SPECIES, :], block_ref.at[:, at : at + SPECIES, :], arrived.at[k]
+        )
+        for k, at in enumerate(range(0, SR, SPECIES))
+    ]
+    for copy in copies:
+        copy.start()
 
     def around(value, by):
         gap = jnp.concatenate([zero] * by, axis=0)
@@ -482,7 +490,9 @@
             [value[by:], gap], axis=0
         )
 
-    for number in range(SPECIES // 8):
+    for number in range(SR // 8):
+        if number * 8 % SPECIES == 0:
+            copies[number * 8 // SPECIES].wait()
         span = slice(number * 8, number * 8 + 8)
         rate = rate_ref[span, :]
         keep = 1.0 - 4.0 * rate
@@ -509,21 +519,20 @@
 
 def diffuse_inside(block, rate):
     tiles = block.shape[0]
-    cells = pl.BlockSpec((tiles, SPECIES, LANES), lambda g: (0, g, 0))
+    vmem = pl.BlockSpec(memory_space=pltpu.VMEM)
     place = np.arange(LANES)
     next_to = (np.abs(place[:, None] - place[None, :]) == 1).astype(np.float32)
     both = np.concatenate([next_to, next_to @ next_to], axis=1)
     both = jnp.asarray(np.concatenate([both, both], axis=0), jnp.bfloat16)
     return pl.pallas_call(
         functools.partial(inner_kernel, tiles),
-        grid=(SR // SPECIES,),
-        in_specs=[
-            cells,
-            pl.BlockSpec((SPECIES, LANES), lambda g: (g, 0)),
-            pl.BlockSpec((2 * LANES, 2 * LANES), lambda g: (0, 0)),
+        in_specs=[pl.BlockSpec(memory_space=pl.ANY), vmem, vmem],
+        out_specs=vmem,
+        out_shape=jax.ShapeDtypeStruct(block.shape, jnp.float32),
+        scratch_shapes=[
+            pltpu.VMEM(block.shape, jnp.float32),
+            pltpu.SemaphoreType.DMA((SR // SPECIES,)),
         ],
-        out_specs=cells,
-        out_shape=jax.ShapeDtypeStruct(block.shape, jnp.float32),
         compiler_params=pltpu.CompilerParams(vmem_limit_bytes=INNER_VMEM),
         cost_estimate=pl.CostEstimate(
             flops=tiles * SR * LANES * 20, bytes_accessed=8 * block.size, transcendentals=0
@@ -680,7 +689,8 @@
     reacted, rows, edge = solve_chunk(1, plan, state, (first, second), early, rows, edge)
 
     near, far = trade(edge, edge, "bal")
-    near_row, far_row = trade(*make_messages(rows, near, far), "box")
+    messages = make_messages(rows.astype(jnp.bfloat16), near, far)
+    near_row, far_row = trade(*messages, "box")
     inner = diffuse_inside(reacted, rate)
     field = add_borders(inner, rows, near_row, far_row, near, far, edge, rate)
     return field.transpose(1, 0, 2)

time: 146 us -> 144 us (0.986)
  starting transfers between devices: 23.8 us -> 13.4 us
  Pallas kernels: 47.8 us -> 57.2 us
  local copies, waits for them, and re-layouts: 2.26 us -> 0.02 us
    pallas_call x2, Pallas kernels: 29.4 us -> 40 us  [solve_chunk(): pl.pallas_call(functools.partial(solve_kernel, chunk), in_specs=in_specs,...]
    ppermute x2, starting transfers between devices: 10.2 us -> 2.71 us  [trade(): lax.ppermute(near_value, axis, near)]
    ppermute x2, starting transfers between devices: 8.33 us -> 5.02 us  [trade(): lax.ppermute(far_value, axis, far)]
    ppermute x2, waiting for transfers between devices: 3.01 us -> 5.66 us  [trade(): lax.ppermute(far_value, axis, far)]
    unnamed x12 -> x8, local copies, waits for them, and re-layouts: 2.26 us -> 0.02 us
  transfers between devices with their start and end apart: 5 -> 5, of which waited for: 3 -> 2; matrix products, arithmetic and copies ran while one was open for 0% -> 1% of each run, Pallas kernels for 17% -> 21%
where the time goes in v1:
time: 144 us; the launch traced here: 143 us
  blocking collectives  65.1 us (45%)
  Pallas kernels  57.2 us (40%)
  starting transfers between devices  13.4 us (9%)
  waiting for transfers between devices  5.67 us (4%)
    all_to_all x1, blocking collectives, exchange(): lax.all_to_all(packed, 'box', split_axis=0, concat_axis=0, tiled=True)  65.1 us
    pallas_call x2, Pallas kernels, solve_chunk(): pl.pallas_call(functools.partial(solve_kernel, chunk), in_specs=in_specs,...  40 us
    pallas_call x1, Pallas kernels, pack_all(): pl.pallas_call(pack_kernel, grid=(boxes // PACK_BOXES,), in_specs=[pl.Blo...  7.91 us
    all_to_all x1, starting transfers between devices, exchange(): lax.all_to_all(packed, 'box', split_axis=0, concat_axis=0, tiled=True)  5.72 us
    ppermute x2, waiting for transfers between devices, trade(): lax.ppermute(far_value, axis, far)  5.66 us
    pallas_call x1, Pallas kernels, add_borders(): pl.pallas_call(functools.partial(border_kernel, tiles), grid=(SR // SPECI...  5.38 us
    ppermute x2, starting transfers between devices, trade(): lax.ppermute(far_value, axis, far)  5.02 us
    pallas_call x1, Pallas kernels, diffuse_inside(): pl.pallas_call(functools.partial(inner_kernel, tiles), in_specs=[pl.Block...  3.71 us
  transfers between devices with their start and end apart: 5, of which 2 were waited for; matrix products, arithmetic and copies ran while one was open for 1% of the time, Pallas kernels for 21%

profile of v1, /device:TPU:66, one launch (start us, length us, event | category | flops | bytes accessed | tf_op | source)
XLA Modules:
  0.0 142.6 jit_solution(13453103317129133672)
XLA Ops:
  0.0 7.9 %pack_all.1 = (s32[8,128]{1,0:T(8,128)}, f32[224,128]{1,0:T(8,128)}, f32[218,32,128]{2,1,0:T(8,128)}, bf16[16,3,400,128]{3,2,1,0:T(8,128)(2,1)}, bf16[16,1,400,128]{3,2,1,0:T(8,128)(2,1)}) custom-call(s32[4,4,64]{2,1,0:T(4,128)} %bitcast.17, s32[4,16]{1,0:T(4,128)} %bitcast.18, s32[1,32]{1,0:T(1,128)} %bitcast.20, f32[1,218]{1,0:T(1,128)} %bitcast.19, ...), custom_call_target="tpu_custom_call" | custom-call | tf_op jit(solution)/shard_map/pack_all/pallas_call | solution.py:146
  7.9 65.1 %all_to_all.10 = bf16[16,3,400,128]{3,2,1,0:T(8,128)(2,1)} all-to-all(bf16[16,3,400,128]{3,2,1,0:T(8,128)(2,1)} %get-tuple-element.26), channel_id=1, replica_groups=mesh['box'=16,'bal'=8] {'box'}, dimensions={0} | all-to-all | bytes 9830400 | tf_op jit(solution)/shard_map/all_to_all | solution.py:680
  73.0 5.7 %all-to-all-start.1 = ((bf16[16,1,400,128]{3,2,1,0:T(8,128)(2,1)}), bf16[16,1,400,128]{3,2,1,0:T(8,128)(2,1)}, u32[]{:S(2)}, u32[]{:S(2)}) async-start(bf16[16,1,400,128]{3,2,1,0:T(8,128)(2,1)} %get-tuple-element.31), calls=%async_computation.1 | async-start | bytes 3276800 | tf_op jit(solution)/shard_map/all_to_all | solution.py:680
  78.7 26.4 %solve_chunk.2 = (f32[32,224,128]{2,1,0:T(8,128)}, f32[4,224,128]{2,1,0:T(8,128)}, f32[224,128]{1,0:T(8,128)}) custom-call(s32[8,128]{1,0:T(8,128)} %get-tuple-element.28.refs_0_, f32[218,32,128]{2,1,0:T(8,128)} %get-tuple-element.29.refs_1_, bf16[48,400,128]{2,1,0:T(8,128)(2,1)} %bitcast.14), custom_call_target="tpu_custom_call" | custom-call | flops 4800000000 | bytes 3200000 | tf_op jit(solution)/shard_map/solve_chunk/pallas_call | solution.py:403
  105.1 0.0 all-to-all-done.1
  105.1 0.0 copy-start.1
  105.2 0.0 copy-start.2
  105.2 13.6 %solve_chunk.3 = (f32[32,224,128]{2,1,0:T(8,128)}, f32[4,224,128]{2,1,0:T(8,128)}, f32[224,128]{1,0:T(8,128)}) custom-call(s32[8,128]{1,0:T(8,128)} %get-tuple-element.28.refs_0_, f32[218,32,128]{2,1,0:T(8,128)} %get-tuple-element.29.refs_1_, bf16[48,400,128]{2,1,0:T(8,128)(2,1)} %bitcast.15, ...), custom_call_target="tpu_custom_call", output_to_operand_aliasing={{0}: (4, {}), {1}: (5, {})} | custom-call | flops 4800000000 | bytes 3200000 | tf_op jit(solution)/shard_map/solve_chunk/pallas_call | solution.py:403
  118.8 1.9 %collective-permute-start.1 = (f32[224,128]{1,0:T(8,128)}, f32[224,128]{1,0:T(8,128)S(1)}, u32[]{:S(2)}, u32[]{:S(2)}) collective-permute-start(f32[224,128]{1,0:T(8,128)} %get-tuple-element.38.own_ref), channel_id=1, source_target_pairs={{1,2},{2,1},{3,4},{4,3},{5,6},{6,5},{9,10},{10,9},{11,12},{12,11},... | collective-permute-start | bytes 344072 | tf_op jit(solution)/shard_map/ppermute | solution.py:661
  120.7 0.6 collective-permute-start
  121.3 1.0 convert_element_type.3.rows_ref
  122.3 2.8 %collective-permute-done.1.far_ref.far_here_ref = f32[224,128]{1,0:T(8,128)S(1)} collective-permute-done((f32[224,128]{1,0:T(8,128)}, f32[224,128]{1,0:T(8,128)S(1)}, u32[]{:S(2)}, u32[]{:S(2)}) %collective-permute-start.1) | collective-permute-done | bytes 114720 | tf_op jit(solution)/shard_map/ppermute | solution.py:661
  125.1 0.0 collective-permute-done.near_ref.near_here_ref
  125.1 0.2 make_messages.1
  125.4 2.1 %collective-permute-start.2 = (bf16[3,224,128]{2,1,0:T(8,128)(2,1)S(1)}, bf16[3,224,128]{2,1,0:T(8,128)(2,1)S(1)}, u32[]{:S(2)}, u32[]{:S(2)}) collective-permute-start(bf16[3,224,128]{2,1,0:T(8,128)(2,1)S(1)} %get-tuple-element.39), channel_id=1, source_target_pairs={{0,8},{8,0},{16,24},{24,16},{32,40},{40,32},{48,56},{56,48},{64,72... | collective-permute-start | bytes 516104 | tf_op jit(solution)/shard_map/ppermute | solution.py:661
  127.5 3.1 %collective-permute-start.3 = (bf16[3,224,128]{2,1,0:T(8,128)(2,1)S(1)}, bf16[3,224,128]{2,1,0:T(8,128)(2,1)S(1)}, u32[]{:S(2)}, u32[]{:S(2)}) collective-permute-start(bf16[3,224,128]{2,1,0:T(8,128)(2,1)S(1)} %get-tuple-element.40), channel_id=1, source_target_pairs={{8,16},{16,8},{24,32},{32,24},{40,48},{48,40},{56,64},{64,56},{72,... | collective-permute-start | bytes 516104 | tf_op jit(solution)/shard_map/ppermute | solution.py:661
  130.6 0.0 copy-done.1
  130.6 0.0 copy-done.2
  130.6 0.0 copy-start
  130.6 0.0 copy-start.3
  130.6 3.7 %diffuse_inside.1.inner_ref = f32[32,224,128]{2,1,0:T(8,128)S(1)} custom-call(f32[32,224,128]{2,1,0:T(8,128)} %get-tuple-element.35.block_hbm, f32[224,128]{1,0:T(8,128)S(1)} %copy-done.1, bf16[256,256]{1,0:T(8,128)(2,1)S(1)} %copy-done.2), custom_call_target="tpu_custom_call" | custom-call | flops 18350080 | bytes 7340032 | tf_op jit(solution)/shard_map/diffuse_inside/pallas_call | solution.py:527
  134.4 0.0 collective-permute-done.2.near_row_ref
  134.4 2.9 %collective-permute-done.3.far_row_ref = bf16[3,224,128]{2,1,0:T(8,128)(2,1)S(1)} collective-permute-done((bf16[3,224,128]{2,1,0:T(8,128)(2,1)S(1)}, bf16[3,224,128]{2,1,0:T(8,128)(2,1)S(1)}, u32[]{:S(2)}, u32[]{:S(2)}) %collective-permute-start.3) | collective-permute-done | bytes 172064 | tf_op jit(solution)/shard_map/ppermute | solution.py:661
  137.3 0.0 copy-done
  137.3 0.0 copy-done.3
  137.3 5.4 %add_borders.1 = f32[218,32,128]{2,1,0:T(8,128)} custom-call(f32[32,224,128]{2,1,0:T(8,128)S(1)} %diffuse_inside.1.inner_ref, f32[4,224,128]{2,1,0:T(8,128)S(1)} %copy-done, f32[4,224,128]{2,1,0:T(8,128)S(1)} %copy-done, bf16[3,224,128]{2,1,0:T(8,128)(2,1)S(1)} %collective-permute-done.2.near_row_ref, ...), custom_call_target="tpu_custom_call" | custom-call | tf_op jit(solution)/shard_map/add_borders/pallas_call | solution.py:634
Async XLA Ops:
  73.0 32.1 %all-to-all-start.1 = ((bf16[16,1,400,128]{3,2,1,0:T(8,128)(2,1)}), bf16[16,1,400,128]{3,2,1,0:T(8,128)(2,1)}, u32[]{:S(2)}, u32[]{:S(2)}) async-start(bf16[16,1,400,128]{3,2,1,0:T(8,128)(2,1)} %get-tuple-element.31), calls=%async_computation.1 | async-start | bytes 3276800 | tf_op jit(solution)/shard_map/all_to_all | solution.py:680
  105.1 25.5 %copy-start.1 = (f32[224,128]{1,0:T(8,128)S(1)}, f32[224,128]{1,0:T(8,128)}, u32[]{:S(2)}) copy-start(f32[224,128]{1,0:T(8,128)} %get-tuple-element.36.rate_ref) | copy-start | bytes 344068
  105.2 25.5 %copy-start.2 = (bf16[256,256]{1,0:T(8,128)(2,1)S(1)}, bf16[256,256]{1,0:T(8,128)(2,1)}, u32[]{:S(2)}) copy-start(bf16[256,256]{1,0:T(8,128)(2,1)} %constant.2.clone.both_ref) | copy-start | bytes 393220
  118.8 6.3 %collective-permute-start.1 = (f32[224,128]{1,0:T(8,128)}, f32[224,128]{1,0:T(8,128)S(1)}, u32[]{:S(2)}, u32[]{:S(2)}) collective-permute-start(f32[224,128]{1,0:T(8,128)} %get-tuple-element.38.own_ref), channel_id=1, source_target_pairs={{1,2},{2,1},{3,4},{4,3},{5,6},{6,5},{9,10},{10,9},{11,12},{12,11},... | collective-permute-start | bytes 344072 | tf_op jit(solution)/shard_map/ppermute | solution.py:661
  120.7 4.4 %collective-permute-start = (f32[224,128]{1,0:T(8,128)}, f32[224,128]{1,0:T(8,128)S(1)}, u32[]{:S(2)}, u32[]{:S(2)}) collective-permute-start(f32[224,128]{1,0:T(8,128)} %get-tuple-element.38.own_ref), channel_id=1, source_target_pairs={{0,1},{1,0},{2,3},{3,2},{4,5},{5,4},{6,7},{7,6},{8,9},{9,8},{10,11... | collective-permute-start | bytes 344072 | tf_op jit(solution)/shard_map/ppermute | solution.py:661
  125.4 9.0 %collective-permute-start.2 = (bf16[3,224,128]{2,1,0:T(8,128)(2,1)S(1)}, bf16[3,224,128]{2,1,0:T(8,128)(2,1)S(1)}, u32[]{:S(2)}, u32[]{:S(2)}) collective-permute-start(bf16[3,224,128]{2,1,0:T(8,128)(2,1)S(1)} %get-tuple-element.39), channel_id=1, source_target_pairs={{0,8},{8,0},{16,24},{24,16},{32,40},{40,32},{48,56},{56,48},{64,72... | collective-permute-start | bytes 516104 | tf_op jit(solution)/shard_map/ppermute | solution.py:661
  127.5 9.8 %collective-permute-start.3 = (bf16[3,224,128]{2,1,0:T(8,128)(2,1)S(1)}, bf16[3,224,128]{2,1,0:T(8,128)(2,1)S(1)}, u32[]{:S(2)}, u32[]{:S(2)}) collective-permute-start(bf16[3,224,128]{2,1,0:T(8,128)(2,1)S(1)} %get-tuple-element.40), channel_id=1, source_target_pairs={{8,16},{16,8},{24,32},{32,24},{40,48},{48,40},{56,64},{64,56},{72,... | collective-permute-start | bytes 516104 | tf_op jit(solution)/shard_map/ppermute | solution.py:661
  130.6 6.6 %copy-start = (f32[4,224,128]{2,1,0:T(8,128)S(1)}, f32[4,224,128]{2,1,0:T(8,128)}, u32[]{:S(2)}) copy-start(f32[4,224,128]{2,1,0:T(8,128)} %get-tuple-element.37.top_ref.bottom_ref) | copy-start | bytes 1376260
  130.6 6.6 %copy-start.3 = (f32[224,128]{1,0:T(8,128)S(1)}, f32[224,128]{1,0:T(8,128)}, u32[]{:S(2)}) copy-start(f32[224,128]{1,0:T(8,128)} %get-tuple-element.38.own_ref) | copy-start | bytes 344068

commit v2 on v1

--- a/solution.py
+++ b/solution.py
@@ -324,12 +324,11 @@
         for member in range(GROUP):
             fetch(places[member], packed_hbm, 0).wait()
             fetch_state(places[member]).wait()
-        for member in range(GROUP):
+        def begin(member):
             unpack(packed, places[member], dense[member])
             start_value = state[places[member]]
             right[member][0:SR, 0:LANES] = start_value.astype(jnp.bfloat16)
             guess[member][...] = start_value
-        for member in range(GROUP):
             remainder = jnp.dot(
                 dense[member][...],
                 right[member][:, 0:LANES],
@@ -340,7 +339,10 @@
 
         half = GROUP // 2
         for member in range(half, GROUP):
-            keep_sums(member, *measure(member, multiply(member)))
+            begin(member)
+        for one, other in zip(range(half), range(half, GROUP)):
+            begin(one)
+            keep_sums(other, *measure(other, multiply(other)))
 
         def advance(turn_no, inner):
             for one, other in zip(range(half), range(half, GROUP)):

time: 144 us -> 143 us (level)
    ppermute x2, starting transfers between devices: 2.71 us -> 1.11 us  [trade(): lax.ppermute(near_value, axis, near)]
    pallas_call x2, Pallas kernels: 40 us -> 38.6 us  [solve_chunk(): pl.pallas_call(functools.partial(solve_kernel, chunk), in_specs=in_specs,...]
  transfers between devices with their start and end apart: 5 -> 5, of which waited for: 2 -> 3; matrix products, arithmetic and copies ran while one was open for 1% -> 1% of each run, Pallas kernels for 21% -> 16%
where the time goes in v2:
time: 143 us; the launch traced here: 141 us
  blocking collectives  65.1 us (46%)
  Pallas kernels  55.8 us (39%)
  starting transfers between devices  12.7 us (9%)
  waiting for transfers between devices  5.8 us (4%)
    all_to_all x1, blocking collectives, exchange(): lax.all_to_all(packed, 'box', split_axis=0, concat_axis=0, tiled=True)  65.1 us
    pallas_call x2, Pallas kernels, solve_chunk(): pl.pallas_call(functools.partial(solve_kernel, chunk), in_specs=in_specs,...  38.6 us
    pallas_call x1, Pallas kernels, pack_all(): pl.pallas_call(pack_kernel, grid=(boxes // PACK_BOXES,), in_specs=[pl.Blo...  7.91 us
    ppermute x2, starting transfers between devices, trade(): lax.ppermute(far_value, axis, far)  5.89 us
    all_to_all x1, starting transfers between devices, exchange(): lax.all_to_all(packed, 'box', split_axis=0, concat_axis=0, tiled=True)  5.72 us
    pallas_call x1, Pallas kernels, add_borders(): pl.pallas_call(functools.partial(border_kernel, tiles), grid=(SR // SPECI...  5.38 us
    ppermute x2, waiting for transfers between devices, trade(): lax.ppermute(far_value, axis, far)  4.37 us
    pallas_call x1, Pallas kernels, diffuse_inside(): pl.pallas_call(functools.partial(inner_kernel, tiles), in_specs=[pl.Block...  3.71 us
  transfers between devices with their start and end apart: 5, of which 3 were waited for; matrix products, arithmetic and copies ran while one was open for 1% of the time, Pallas kernels for 16%

profile of v2, /device:TPU:66, one launch (start us, length us, event | category | flops | bytes accessed | tf_op | source)
XLA Modules:
  0.0 140.6 jit_solution(2720736750294561924)
XLA Ops:
  0.0 7.9 %pack_all.1 = (s32[8,128]{1,0:T(8,128)}, f32[224,128]{1,0:T(8,128)}, f32[218,32,128]{2,1,0:T(8,128)}, bf16[16,3,400,128]{3,2,1,0:T(8,128)(2,1)}, bf16[16,1,400,128]{3,2,1,0:T(8,128)(2,1)}) custom-call(s32[4,4,64]{2,1,0:T(4,128)} %bitcast.17, s32[4,16]{1,0:T(4,128)} %bitcast.18, s32[1,32]{1,0:T(1,128)} %bitcast.20, f32[1,218]{1,0:T(1,128)} %bitcast.19, ...), custom_call_target="tpu_custom_call" | custom-call | tf_op jit(solution)/shard_map/pack_all/pallas_call | solution.py:146
  7.9 65.1 %all_to_all.10 = bf16[16,3,400,128]{3,2,1,0:T(8,128)(2,1)} all-to-all(bf16[16,3,400,128]{3,2,1,0:T(8,128)(2,1)} %get-tuple-element.26), channel_id=1, replica_groups=mesh['box'=16,'bal'=8] {'box'}, dimensions={0} | all-to-all | bytes 9830400 | tf_op jit(solution)/shard_map/all_to_all | solution.py:682
  73.0 5.7 %all-to-all-start.1 = ((bf16[16,1,400,128]{3,2,1,0:T(8,128)(2,1)}), bf16[16,1,400,128]{3,2,1,0:T(8,128)(2,1)}, u32[]{:S(2)}, u32[]{:S(2)}) async-start(bf16[16,1,400,128]{3,2,1,0:T(8,128)(2,1)} %get-tuple-element.31), calls=%async_computation.1 | async-start | bytes 3276800 | tf_op jit(solution)/shard_map/all_to_all | solution.py:682
  78.7 19.4 %solve_chunk.2 = (f32[32,224,128]{2,1,0:T(8,128)}, f32[4,224,128]{2,1,0:T(8,128)}, f32[224,128]{1,0:T(8,128)}) custom-call(s32[8,128]{1,0:T(8,128)} %get-tuple-element.28.refs_0_, f32[218,32,128]{2,1,0:T(8,128)} %get-tuple-element.29.refs_1_, bf16[48,400,128]{2,1,0:T(8,128)(2,1)} %bitcast.14), custom_call_target="tpu_custom_call" | custom-call | flops 4800000000 | bytes 3200000 | tf_op jit(solution)/shard_map/solve_chunk/pallas_call | solution.py:405
  98.2 1.4 %all-to-all-done.1 = bf16[16,1,400,128]{3,2,1,0:T(8,128)(2,1)} async-done(((bf16[16,1,400,128]{3,2,1,0:T(8,128)(2,1)}), bf16[16,1,400,128]{3,2,1,0:T(8,128)(2,1)}, u32[]{:S(2)}, u32[]{:S(2)}) %all-to-all-start.1) | async-done | bytes 1638432 | tf_op jit(solution)/shard_map/all_to_all | solution.py:682
  99.6 0.0 copy-start.1
  99.6 0.0 copy-start.2
  99.6 19.1 %solve_chunk.3 = (f32[32,224,128]{2,1,0:T(8,128)}, f32[4,224,128]{2,1,0:T(8,128)}, f32[224,128]{1,0:T(8,128)}) custom-call(s32[8,128]{1,0:T(8,128)} %get-tuple-element.28.refs_0_, f32[218,32,128]{2,1,0:T(8,128)} %get-tuple-element.29.refs_1_, bf16[48,400,128]{2,1,0:T(8,128)(2,1)} %bitcast.15, ...), custom_call_target="tpu_custom_call", output_to_operand_aliasing={{0}: (4, {}), {1}: (5, {})} | custom-call | flops 4800000000 | bytes 3200000 | tf_op jit(solution)/shard_map/solve_chunk/pallas_call | solution.py:405
  118.7 1.9 %collective-permute-start.1 = (f32[224,128]{1,0:T(8,128)}, f32[224,128]{1,0:T(8,128)S(1)}, u32[]{:S(2)}, u32[]{:S(2)}) collective-permute-start(f32[224,128]{1,0:T(8,128)} %get-tuple-element.38.own_ref), channel_id=1, source_target_pairs={{1,2},{2,1},{3,4},{4,3},{5,6},{6,5},{9,10},{10,9},{11,12},{12,11},... | collective-permute-start | bytes 344072 | tf_op jit(solution)/shard_map/ppermute | solution.py:663
  120.7 1.0 collective-permute-start
  121.7 1.0 convert_element_type.3.rows_ref
  122.8 2.3 %collective-permute-done.1.far_ref.far_here_ref = f32[224,128]{1,0:T(8,128)S(1)} collective-permute-done((f32[224,128]{1,0:T(8,128)}, f32[224,128]{1,0:T(8,128)S(1)}, u32[]{:S(2)}, u32[]{:S(2)}) %collective-permute-start.1) | collective-permute-done | bytes 114720 | tf_op jit(solution)/shard_map/ppermute | solution.py:663
  125.1 0.0 collective-permute-done.near_ref.near_here_ref
  125.1 0.2 make_messages.1
  125.3 0.1 collective-permute-start.2
  125.4 4.0 %collective-permute-start.3 = (bf16[3,224,128]{2,1,0:T(8,128)(2,1)S(1)}, bf16[3,224,128]{2,1,0:T(8,128)(2,1)S(1)}, u32[]{:S(2)}, u32[]{:S(2)}) collective-permute-start(bf16[3,224,128]{2,1,0:T(8,128)(2,1)S(1)} %get-tuple-element.40), channel_id=1, source_target_pairs={{8,16},{16,8},{24,32},{32,24},{40,48},{48,40},{56,64},{64,56},{72,... | collective-permute-start | bytes 516104 | tf_op jit(solution)/shard_map/ppermute | solution.py:663
  129.4 0.0 copy-done.1
  129.4 0.0 copy-done.2
  129.4 0.0 copy-start
  129.4 0.0 copy-start.3
  129.4 3.7 %diffuse_inside.1.inner_ref = f32[32,224,128]{2,1,0:T(8,128)S(1)} custom-call(f32[32,224,128]{2,1,0:T(8,128)} %get-tuple-element.35.block_hbm, f32[224,128]{1,0:T(8,128)S(1)} %copy-done.1, bf16[256,256]{1,0:T(8,128)(2,1)S(1)} %copy-done.2), custom_call_target="tpu_custom_call" | custom-call | flops 18350080 | bytes 7340032 | tf_op jit(solution)/shard_map/diffuse_inside/pallas_call | solution.py:529
  133.1 0.0 collective-permute-done.2.near_row_ref
  133.1 2.1 %collective-permute-done.3.far_row_ref = bf16[3,224,128]{2,1,0:T(8,128)(2,1)S(1)} collective-permute-done((bf16[3,224,128]{2,1,0:T(8,128)(2,1)S(1)}, bf16[3,224,128]{2,1,0:T(8,128)(2,1)S(1)}, u32[]{:S(2)}, u32[]{:S(2)}) %collective-permute-start.3) | collective-permute-done | bytes 172064 | tf_op jit(solution)/shard_map/ppermute | solution.py:663
  135.2 0.0 copy-done
  135.2 0.0 copy-done.3
  135.2 5.4 %add_borders.1 = f32[218,32,128]{2,1,0:T(8,128)} custom-call(f32[32,224,128]{2,1,0:T(8,128)S(1)} %diffuse_inside.1.inner_ref, f32[4,224,128]{2,1,0:T(8,128)S(1)} %copy-done, f32[4,224,128]{2,1,0:T(8,128)S(1)} %copy-done, bf16[3,224,128]{2,1,0:T(8,128)(2,1)S(1)} %collective-permute-done.2.near_row_ref, ...), custom_call_target="tpu_custom_call" | custom-call | tf_op jit(solution)/shard_map/add_borders/pallas_call | solution.py:636
Async XLA Ops:
  73.0 26.6 %all-to-all-start.1 = ((bf16[16,1,400,128]{3,2,1,0:T(8,128)(2,1)}), bf16[16,1,400,128]{3,2,1,0:T(8,128)(2,1)}, u32[]{:S(2)}, u32[]{:S(2)}) async-start(bf16[16,1,400,128]{3,2,1,0:T(8,128)(2,1)} %get-tuple-element.31), calls=%async_computation.1 | async-start | bytes 3276800 | tf_op jit(solution)/shard_map/all_to_all | solution.py:682
  99.6 29.8 %copy-start.1 = (f32[224,128]{1,0:T(8,128)S(1)}, f32[224,128]{1,0:T(8,128)}, u32[]{:S(2)}) copy-start(f32[224,128]{1,0:T(8,128)} %get-tuple-element.36.rate_ref) | copy-start | bytes 344068
  99.6 29.8 %copy-start.2 = (bf16[256,256]{1,0:T(8,128)(2,1)S(1)}, bf16[256,256]{1,0:T(8,128)(2,1)}, u32[]{:S(2)}) copy-start(bf16[256,256]{1,0:T(8,128)(2,1)} %constant.2.clone.both_ref) | copy-start | bytes 393220
  118.7 6.3 %collective-permute-start.1 = (f32[224,128]{1,0:T(8,128)}, f32[224,128]{1,0:T(8,128)S(1)}, u32[]{:S(2)}, u32[]{:S(2)}) collective-permute-start(f32[224,128]{1,0:T(8,128)} %get-tuple-element.38.own_ref), channel_id=1, source_target_pairs={{1,2},{2,1},{3,4},{4,3},{5,6},{6,5},{9,10},{10,9},{11,12},{12,11},... | collective-permute-start | bytes 344072 | tf_op jit(solution)/shard_map/ppermute | solution.py:663
  120.7 4.4 %collective-permute-start = (f32[224,128]{1,0:T(8,128)}, f32[224,128]{1,0:T(8,128)S(1)}, u32[]{:S(2)}, u32[]{:S(2)}) collective-permute-start(f32[224,128]{1,0:T(8,128)} %get-tuple-element.38.own_ref), channel_id=1, source_target_pairs={{0,1},{1,0},{2,3},{3,2},{4,5},{5,4},{6,7},{7,6},{8,9},{9,8},{10,11... | collective-permute-start | bytes 344072 | tf_op jit(solution)/shard_map/ppermute | solution.py:663
  125.3 7.8 %collective-permute-start.2 = (bf16[3,224,128]{2,1,0:T(8,128)(2,1)S(1)}, bf16[3,224,128]{2,1,0:T(8,128)(2,1)S(1)}, u32[]{:S(2)}, u32[]{:S(2)}) collective-permute-start(bf16[3,224,128]{2,1,0:T(8,128)(2,1)S(1)} %get-tuple-element.39), channel_id=1, source_target_pairs={{0,8},{8,0},{16,24},{24,16},{32,40},{40,32},{48,56},{56,48},{64,72... | collective-permute-start | bytes 516104 | tf_op jit(solution)/shard_map/ppermute | solution.py:663
  125.4 9.8 %collective-permute-start.3 = (bf16[3,224,128]{2,1,0:T(8,128)(2,1)S(1)}, bf16[3,224,128]{2,1,0:T(8,128)(2,1)S(1)}, u32[]{:S(2)}, u32[]{:S(2)}) collective-permute-start(bf16[3,224,128]{2,1,0:T(8,128)(2,1)S(1)} %get-tuple-element.40), channel_id=1, source_target_pairs={{8,16},{16,8},{24,32},{32,24},{40,48},{48,40},{56,64},{64,56},{72,... | collective-permute-start | bytes 516104 | tf_op jit(solution)/shard_map/ppermute | solution.py:663
  129.4 5.8 %copy-start = (f32[4,224,128]{2,1,0:T(8,128)S(1)}, f32[4,224,128]{2,1,0:T(8,128)}, u32[]{:S(2)}) copy-start(f32[4,224,128]{2,1,0:T(8,128)} %get-tuple-element.37.top_ref.bottom_ref) | copy-start | bytes 1376260
  129.4 5.8 %copy-start.3 = (f32[224,128]{1,0:T(8,128)S(1)}, f32[224,128]{1,0:T(8,128)}, u32[]{:S(2)}) copy-start(f32[224,128]{1,0:T(8,128)} %get-tuple-element.38.own_ref) | copy-start | bytes 344068
